TPU v7x, 32 devices: a whole 2x2x4 slice. The times are simulated.
32 devices in a mesh: parts: 2 (over y), grp: 4 (over z), fsdp: 4 (over x, core).
Axes of the slice: x: 2, y: 2, z: 4, core: 2. Of those that a mesh axis runs over, the one named last changes fastest.
Arguments:
- tokens: bfloat16 [4096, 8192], P(('parts', 'grp'), 'fsdp'), parts along dimension 0, may hold values from -6 to 6
- value_matrix: bfloat16 [8192, 512], P(('fsdp', 'grp')), may hold values from -0.0625 to 0.0625
- adapter_down_factors: bfloat16 [16, 64, 8192], P('grp', None, 'fsdp'), may hold values from -0.0625 to 0.0625
- adapter_up_factors: bfloat16 [16, 64, 512], P('grp', None, 'fsdp'), may hold values from -0.75 to 0.75
- block_adapter_index: int32 [32], P('parts'), parts along dimension 0, may hold values from 0 to 15, as said below
- cotangent_feature_major: bfloat16 [512, 4096], P('fsdp', ('parts', 'grp')), parts along dimension 1, may hold values from -0.59765625 to 0.59765625
Outputs:
- values_feature_major: bfloat16 [512, 4096], P('fsdp', ('parts', 'grp')), parts along dimension 1
- tokens_grad: bfloat16 [4096, 8192], P(('parts', 'grp'), 'fsdp'), parts along dimension 0
- down_grad: bfloat16 [32, 64, 8192], P(('parts', 'grp'), None, 'fsdp'), parts along dimension 0
- up_grad: float32 [32, 64, 512], P(('parts', 'grp'), None, 'fsdp'), parts along dimension 0
There are 2 independent parts, one for each index of `parts`. A program takes and returns all parts, laid end to end along the dimension named above; an argument that names none is the same for every part. Nothing has to cross between parts.
Inputs may be any that keep to these rules, and one draw needn't show every extreme that they name: `block_adapter_index`: within the blocks of one group (each run of 4 entries), at most 2 distinct adapters share one owner a // 4, and every group uses exactly 2 of some owner.
All inputs are finite; a program needn't handle non-finite values.
Results may differ from a plain program's by a relative error of at most 0.0049.
Values may be sent and summed in bfloat16 or wider, within the bound.
A program may use at most 128 MiB of HBM per device.

v0:
```python
import jax
import jax.numpy as jnp
from jax import lax
from jax.sharding import PartitionSpec as P

CAP = 2
BLK = 128


adapter_scale = 0.5


def slot_tables(block_adapter_index, groups, per_owner_group, blocks_grp):
    table = block_adapter_index.reshape(groups, blocks_grp)
    adapters = groups * per_owner_group
    hits = table[:, :, None] == jnp.arange(adapters, dtype=jnp.int32)[None, None, :]
    used = jnp.any(hits, axis=1).reshape(groups, groups, per_owner_group).astype(jnp.int32)
    ranked = jnp.cumsum(used, axis=2) - used
    return (table, used, ranked)


def on_device(
    tokens,
    value_matrix,
    adapter_down_factors,
    adapter_up_factors,
    block_adapter_index,
    cotangent_feature_major,
):
    groups = lax.axis_size("grp")
    here = lax.axis_index("grp")
    group_rows, dcols = tokens.shape
    per_owner_group = adapter_down_factors.shape[0]
    rank_extent = adapter_down_factors.shape[1]
    key_value_columns = adapter_up_factors.shape[2]
    blocks_grp = group_rows // BLK
    places = groups * CAP
    table, used, ranked = slot_tables(block_adapter_index, groups, per_owner_group, blocks_grp)
    mine = lax.dynamic_index_in_dim(table, here, 0, keepdims=False)
    my_ranked = lax.dynamic_index_in_dim(ranked, here, 0, keepdims=False).reshape(-1)
    position = mine // per_owner_group * CAP + my_ranked[mine]
    to_slot = (position[:, None] == jnp.arange(places, dtype=jnp.int32)[None, :]).astype(
        jnp.float32
    )
    own_used = lax.dynamic_index_in_dim(used, here, 1, keepdims=False)
    own_ranked = lax.dynamic_index_in_dim(ranked, here, 1, keepdims=False)
    select = (own_ranked[:, None, :] == jnp.arange(CAP, dtype=jnp.int32)[None, :, None]) & (
        own_used[:, None, :] > 0
    )
    weight_rows = lax.all_gather(value_matrix, "grp", axis=0, tiled=True)
    stock_down, stock_up = (
        lax.all_gather(adapter_down_factors, "grp", axis=0, tiled=True),
        lax.all_gather(adapter_up_factors, "grp", axis=0, tiled=True),
    )
    down_blocks = jnp.take(stock_down, mine, axis=0)
    up_blocks = jnp.take(stock_up, mine, axis=0)
    token_blocks = tokens.reshape(blocks_grp, BLK, dcols)
    columns = weight_rows
    base_output_major = lax.psum_scatter(
        lax.dot_general(
            columns, tokens, (((0,), (1,)), ((), ())), preferred_element_type=jnp.float32
        ),
        "fsdp",
        scatter_dimension=0,
        tiled=True,
    )
    low_part = lax.dot_general(
        down_blocks, token_blocks, (((2,), (2,)), ((0,), (0,))), preferred_element_type=jnp.float32
    )
    low_rank_state = lax.psum(low_part, "fsdp").astype(jnp.bfloat16)
    adapter_output = lax.dot_general(
        up_blocks, low_rank_state, (((1,), (1,)), ((0,), (0,))), preferred_element_type=jnp.float32
    )
    adapter_output_major = jnp.transpose(adapter_output, (1, 0, 2)).reshape(
        key_value_columns, group_rows
    )
    values_feature_major = (base_output_major + adapter_scale * adapter_output_major).astype(
        jnp.bfloat16
    )
    cot_blocks = cotangent_feature_major.reshape(key_value_columns, blocks_grp, BLK)
    backward_piece = adapter_scale * lax.dot_general(
        up_blocks, cot_blocks, (((2,), (0,)), ((0,), (1,))), preferred_element_type=jnp.float32
    )
    backward_pass = lax.psum(backward_piece, "fsdp").astype(jnp.bfloat16)
    columns = weight_rows
    grad_base = lax.dot_general(
        lax.all_gather(cotangent_feature_major, "fsdp", axis=0, tiled=True),
        columns,
        (((0,), (1,)), ((), ())),
        preferred_element_type=jnp.float32,
    )
    grad_low = lax.dot_general(
        backward_pass, down_blocks, (((1,), (1,)), ((0,), (0,))), preferred_element_type=jnp.float32
    )
    tokens_grad = (grad_base + grad_low.reshape(group_rows, dcols)).astype(jnp.bfloat16)
    down_part = lax.dot_general(
        backward_pass,
        token_blocks,
        (((2,), (1,)), ((0,), (0,))),
        preferred_element_type=jnp.float32,
    )
    up_piece = adapter_scale * lax.dot_general(
        low_rank_state, cot_blocks, (((2,), (2,)), ((0,), (1,))), preferred_element_type=jnp.float32
    )
    down_slots = jnp.einsum("bp,brd->prd", to_slot, down_part, precision=lax.Precision.HIGHEST)
    up_slots = jnp.einsum("bp,brk->prk", to_slot, up_piece, precision=lax.Precision.HIGHEST)
    slot_down = down_slots.reshape(groups, CAP, rank_extent, dcols)
    slot_up = up_slots.reshape(groups, CAP, rank_extent, key_value_columns)
    got_grad_down, got_grad_up = (
        lax.all_to_all(slot_down, "grp", split_axis=0, concat_axis=0, tiled=True),
        lax.all_to_all(slot_up, "grp", split_axis=0, concat_axis=0, tiled=True),
    )
    collector = select.astype(jnp.float32)
    down_grad = jnp.einsum(
        "gcj,gcrd->jrd", collector, got_grad_down, precision=lax.Precision.HIGHEST
    ).astype(jnp.bfloat16)
    up_grad = jnp.einsum("gcj,gcrk->jrk", collector, got_grad_up, precision=lax.Precision.HIGHEST)
    return (values_feature_major, tokens_grad, down_grad, up_grad)


def solution(mesh):
    return jax.shard_map(
        on_device,
        mesh=mesh,
        in_specs=(
            P(("parts", "grp"), "fsdp"),
            P(("fsdp", "grp"), None),
            P("grp", None, "fsdp"),
            P("grp", None, "fsdp"),
            P("parts"),
            P("fsdp", ("parts", "grp")),
        ),
        out_specs=(
            P("fsdp", ("parts", "grp")),
            P(("parts", "grp"), "fsdp"),
            P(("parts", "grp"), None, "fsdp"),
            P(("parts", "grp"), None, "fsdp"),
        ),
        check_vma=False,
    )
```

profile of v0, /device:TPU:0, one launch (start us, length us, event | category | flops | bytes accessed | tf_op | source)
XLA Modules:
  0.0 252.3 jit_solution(13475612066737129197)
XLA Ops:
  7.2 0.0 copy-start
  7.2 0.0 copy-start.3
  7.2 0.0 all-gather.5.cloned.1.call-start
  7.2 0.7 all-gather.5.cloned.1.call-update
  7.9 0.0 all-gather.3.cloned.1.call-start
  8.0 0.7 all-gather.3.cloned.1.call-update
  8.7 0.7 reshape.101
  9.4 0.0 copy-start.6
  9.5 0.1 fusion.25
  9.5 16.5 %all_gather.13 = bf16[16,64,128]{2,1,0:T(8,128)(2,1)S(1)} all-gather(bf16[4,64,128]{2,1,0:T(8,128)(2,1)} %param.9), channel_id=1, replica_groups=mesh['parts'=2,'grp'=4,'fsdp'=4] {'grp'}, dimensions={0}, use_global_device_ids=true | all-gather | bytes 327680 | tf_op jit(solution)/shard_map/all_gather | solution.py:53
  26.0 0.6 gather_fusion
  26.6 0.0 copy-done.3
  26.6 0.0 copy-start.4
  26.6 0.2 convolution_multiply_fusion.2
  26.9 0.1 reshape.108
  26.9 0.7 reduce_window_sum.11
  27.6 0.0 copy-done.4
  27.7 0.1 reshape.105
  27.7 0.6 gather_fusion.2
  28.4 0.0 copy-start.8
  28.4 65.3 %all-gather.5.cloned.1.call-done = bf16[16,64,2048]{2,1,0:T(8,128)(2,1)} async-done(((bf16[4,64,2048]{2,1,0:T(8,128)(2,1)}), bf16[16,64,2048]{2,1,0:T(8,128)(2,1)}) %all-gather.5.cloned.1.call-update) | async-done | bytes 4194320 | tf_op jit(solution)/shard_map/all_gather | solution.py:52
  93.7 2.8 %gather_fusion.1 = bf16[4,64,2048]{2,1,0:T(8,128)(2,1)S(1)} fusion(bf16[16,64,2048]{2,1,0:T(8,128)(2,1)} %all-gather.5.cloned.1.call-done, s32[1024]{0:T(1024)S(1)} %pad_clamp_fusion), kind=kCustom, calls=%fused_computation.1 | custom fusion | bytes 2097168 | tf_op jit(solution)/shard_map/jit(_take)/gather | solution.py:55
  96.5 0.0 copy-done
  96.5 0.0 copy-done.6
  96.5 1.5 fusion.12
  98.1 15.4 %all-reduce.2 = (bf16[4,64,128]{2,1,0:T(8,128)(2,1)S(1)}, bf16[4,64,128]{2,1,0:T(8,128)(2,1)}) all-reduce(f32[4,64,128]{2,1,0:T(8,128)} %fusion.12, f32[4,64,128]{2,1,0:T(8,128)S(1)} %convolution_multiply_fusion.2), channel_id=1, replica_groups=mesh['parts'=2,'grp'=4,'fsdp'=4] {'fsdp'}, use_global_device_ids=true, to_apply=%region_1.0 | all-reduce | flops 65536 | bytes 393216 | tf_op jit(solution)/shard_map/psum | solution.py:70
  113.5 0.0 copy-start.5
  113.5 0.2 convolution_multiply_fusion.1
  113.6 0.0 copy-done.8
  113.7 0.4 fusion.16
  114.1 0.8 copy.50
  114.9 0.0 copy-done.5
  114.9 3.4 %all-to-all-start.1 = ((f32[4,2,64,128]{3,1,2,0:T(2,128)}), f32[4,2,64,128]{3,1,2,0:T(2,128)S(1)}, u32[]{:S(2)}, u32[]{:S(2)}) async-start(f32[4,2,64,128]{3,1,2,0:T(2,128)} %copy.50), calls=%async_computation.2 | async-start | bytes 524288 | tf_op jit(solution)/shard_map/all_to_all | solution.py:111
  118.3 0.0 copy-start.9
  118.3 1.3 fusion.41
  119.6 0.0 copy-done.9
  119.6 4.8 %fusion.9 = f32[8,64,2048]{2,0,1:T(8,128)} fusion(f32[4,64,2048]{2,1,0:T(8,128)S(1)} %fusion.41, s32[4]{0:T(128)S(1)} %copy-done.9), kind=kOutput, calls=%fused_computation.9 | convolution fusion | flops 50331680 | bytes 6291472 | tf_op jit(solution)/shard_map/bp,brd->prd/dot_general | solution.py:105
  124.4 5.9 %reshape.106 = f32[4,2,64,2048]{3,1,0,2:T(2,128)} reshape(f32[8,64,2048]{2,0,1:T(8,128)} %fusion.9) | data formatting | bytes 8388608 | tf_op jit(solution)/shard_map/reshape | solution.py:107
  130.2 6.7 %copy.46 = f32[4,2,64,2048]{3,1,2,0:T(2,128)} copy(f32[4,2,64,2048]{3,1,0,2:T(2,128)} %reshape.106) | data formatting | bytes 8388608 | tf_op jit(solution)/shard_map/reshape | solution.py:107
  136.9 0.0 all-to-all-done.1
  136.9 5.1 %all-to-all-start = ((f32[4,2,64,2048]{3,1,2,0:T(2,128)}), f32[4,2,64,2048]{3,1,2,0:T(2,128)}, u32[]{:S(2)}, u32[]{:S(2)}) async-start(f32[4,2,64,2048]{3,1,2,0:T(2,128)} %copy.46), calls=%async_computation.1 | async-start | bytes 8388608 | tf_op jit(solution)/shard_map/all_to_all | solution.py:110
  142.0 0.0 reduce-scatter.2.cloned.1.call-start
  142.0 3.3 %all-gather.3.cloned.1.call-done = bf16[2048,512]{1,0:T(8,128)(2,1)} async-done(((bf16[512,512]{1,0:T(8,128)(2,1)}), bf16[2048,512]{1,0:T(8,128)(2,1)}) %all-gather.3.cloned.1.call-update) | async-done | bytes 2097168 | tf_op jit(solution)/shard_map/all_gather | solution.py:50
  145.3 3.9 %fusion.40 = f32[512,512]{1,0:T(8,128)} fusion(bf16[2048,512]{1,0:T(8,128)(2,1)} %all-gather.3.cloned.1.call-done, bf16[512,2048]{1,0:T(8,128)(2,1)S(1)} %copy-done), kind=kOutput, calls=%fused_computation.60 | convolution fusion | flops 1073741824 | bytes 5242880 | tf_op jit(solution)/shard_map/dot_general | solution.py:60
  149.1 0.0 reduce-scatter.2.cloned.1.call-update
  149.1 0.6 constant_dynamic-slice_fusion.1
  149.7 0.8 copy.43
  150.5 0.0 copy-start.7
  150.5 0.1 copy.57
  150.6 28.5 %all_gather.15 = bf16[512,512]{1,0:T(8,128)(2,1)} all-gather(bf16[128,512]{1,0:T(8,128)(2,1)S(1)} %copy-done.3), channel_id=1, replica_groups=mesh['parts'=2,'grp'=4,'fsdp'=4] {'fsdp'}, dimensions={0}, use_global_device_ids=true | all-gather | bytes 655360 | tf_op jit(solution)/shard_map/all_gather | solution.py:87
  179.1 1.8 convolution_multiply_fusion
  180.9 1.8 copy.56
  182.7 10.2 %reduce-scatter.2.cloned.1.call-done = f32[128,512]{1,0:T(8,128)} async-done(((f32[512,512]{1,0:T(8,128)}), f32[128,512]{1,0:T(8,128)}) %reduce-scatter.2.cloned.1.call-update) | async-done | bytes 262160 | tf_op jit(solution)/shard_map/reduce_scatter | solution.py:59
  192.9 1.7 add_convert_fusion
  194.6 0.0 copy-done.7
  194.6 1.8 fusion.11
  196.4 0.0 copy-done.1
  196.4 0.0 copy-done.2
  196.4 2.6 %fusion = bf16[512,2048]{1,0:T(8,128)(2,1)} fusion(f32[4,128,2048]{2,1,0:T(8,128)S(1)} %fusion.11, bf16[512,512]{1,0:T(8,128)(2,1)S(1)} %copy-done.2, bf16[2048,512]{1,0:T(8,128)(2,1)S(1)} %copy-done.1), kind=kOutput, calls=%fused_computation.4 | convolution fusion | flops 1075838976 | bytes 8912896 | tf_op jit(solution)/shard_map/dot_general | solution.py:86
  199.0 0.5 convolution_bitcast_fusion
  199.5 0.7 copy.53
  200.2 35.0 %all-to-all-done = f32[4,2,64,2048]{3,1,2,0:T(2,128)} async-done(((f32[4,2,64,2048]{3,1,2,0:T(2,128)}), f32[4,2,64,2048]{3,1,2,0:T(2,128)}, u32[]{:S(2)}, u32[]{:S(2)}) %all-to-all-start) | async-done | bytes 4194336 | tf_op jit(solution)/shard_map/all_to_all | solution.py:110
  235.3 8.9 %fusion.6 = bf16[4,64,2048]{2,0,1:T(4,128)(2,1)S(1)} fusion(f32[4,2,64,2048]{3,1,2,0:T(2,128)} %all-to-all-done, s32[4,4]{0,1:T(4,128)S(1)} %copy.43, pred[4,4]{0,1:T(4,128)(4,1)S(1)} %bitcast.72), kind=kOutput, calls=%fused_computation.8 | convolution fusion | flops 50856000 | bytes 5242960 | tf_op jit(solution)/shard_map/gcj,gcrd->jrd/dot_general | solution.py:114
  244.2 1.5 copy.52
  (10 shorter events, 0.1 us)
Async XLA Ops:
  7.2 89.3 %copy-start = (bf16[512,2048]{1,0:T(8,128)(2,1)S(1)}, bf16[512,2048]{1,0:T(8,128)(2,1)}, u32[]{:S(2)}) copy-start(bf16[512,2048]{1,0:T(8,128)(2,1)} %param.6) | copy-start | bytes 6291460
  7.2 19.4 %copy-start.3 = (bf16[128,512]{1,0:T(8,128)(2,1)S(1)}, bf16[128,512]{1,0:T(8,128)(2,1)}, u32[]{:S(2)}) copy-start(bf16[128,512]{1,0:T(8,128)(2,1)} %param.11) | copy-start | bytes 393220
  7.2 86.5 %all-gather.5.cloned.1.call-start = ((), (), s32[]{:S(2)}) async-start(), calls=%async_computation.5 | async-start | bytes 5242880 | tf_op jit(solution)/shard_map/all_gather | solution.py:52
  7.9 137.3 %all-gather.3.cloned.1.call-start = ((), (), s32[]{:S(2)}) async-start(), calls=%async_computation.3 | async-start | bytes 2621440 | tf_op jit(solution)/shard_map/all_gather | solution.py:50
  9.4 87.1 %copy-start.6 = (pred[4]{0:T(512)(128)(4,1)}, pred[4]{0:T(512)(128)(4,1)S(1)}, u32[]{:S(2)}) copy-start(pred[4]{0:T(512)(128)(4,1)S(1)} %compare_and_fusion) | copy-start | bytes 16
  26.6 1.0 copy-start.4
  28.4 85.3 %copy-start.8 = (s32[4]{0:T(128)}, s32[4]{0:T(128)S(1)}, u32[]{:S(2)}) copy-start(s32[4]{0:T(128)S(1)} %multiply_add_fusion) | copy-start | bytes 52
  113.5 1.4 copy-start.5
  114.9 22.0 %all-to-all-start.1 = ((f32[4,2,64,128]{3,1,2,0:T(2,128)}), f32[4,2,64,128]{3,1,2,0:T(2,128)S(1)}, u32[]{:S(2)}, u32[]{:S(2)}) async-start(f32[4,2,64,128]{3,1,2,0:T(2,128)} %copy.50), calls=%async_computation.2 | async-start | bytes 524288 | tf_op jit(solution)/shard_map/all_to_all | solution.py:111
  118.3 1.3 copy-start.9
  136.9 98.3 %all-to-all-start = ((f32[4,2,64,2048]{3,1,2,0:T(2,128)}), f32[4,2,64,2048]{3,1,2,0:T(2,128)}, u32[]{:S(2)}, u32[]{:S(2)}) async-start(f32[4,2,64,2048]{3,1,2,0:T(2,128)} %copy.46), calls=%async_computation.1 | async-start | bytes 8388608 | tf_op jit(solution)/shard_map/all_to_all | solution.py:110
  142.0 50.9 %reduce-scatter.2.cloned.1.call-start = ((), (), s32[]{:S(2)}) async-start(), calls=%async_computation.4 | async-start | bytes 1310720 | tf_op jit(solution)/shard_map/reduce_scatter | solution.py:59
  150.5 44.1 %copy-start.7 = (pred[4]{0:T(512)(128)(4,1)S(1)}, pred[4]{0:T(512)(128)(4,1)}, u32[]{:S(2)}) copy-start(pred[4]{0:T(512)(128)(4,1)} %copy-done.6) | copy-start | bytes 16
  194.6 1.8 copy-start.1
  194.6 1.8 copy-start.2
Sparse Core Ops, SparseCore 0:
  9.6 84.0 all-gather.4
  95.3 49.9 all-gather.2
  149.3 43.6 reduce-scatter.1
where the time goes:
time: 253 us; the launch traced here: 252 us
  waiting for transfers between devices  115 us (45%)
  blocking collectives  60.4 us (24%)
  matrix products  27.8 us (11%)
  local copies, waits for them, and re-layouts  23.8 us (9%)
  between operations  13.9 us (5%)
  starting transfers between devices  8.54 us (3%)
  other arithmetic  2.56 us (1%)
    all_gather x1, waiting for transfers between devices, on_device(): lax.all_gather(adapter_down_factors, 'grp', axis=0, tiled=True)  65.3 us
    all_to_all x1, waiting for transfers between devices, on_device(): lax.all_to_all(slot_down, 'grp', split_axis=0, concat_axis=0, tiled=True)  35 us
    all_gather x1, blocking collectives, on_device(): lax.all_gather(cotangent_feature_major, 'fsdp', axis=0, tiled=True)  28.5 us
    all_gather x1, blocking collectives, on_device(): lax.all_gather(adapter_up_factors, 'grp', axis=0, tiled=True)  16.5 us
    psum x1, blocking collectives, on_device(): low_rank_state = lax.psum(low_part, 'fsdp').astype(jnp.bfloat16)  15.4 us
    reshape x2, local copies, waits for them, and re-layouts, on_device(): slot_down = down_slots.reshape(groups, CAP, rank_extent, dcols)  12.6 us
    reduce_scatter x1, waiting for transfers between devices, on_device(): lax.psum_scatter(lax.dot_general(columns, tokens, (((0,), (1,)), ((), ())...  10.2 us
    dot_general x1, matrix products, on_device(): jnp.einsum('gcj,gcrd->jrd', collector, got_grad_down, precision=lax.Preci...  8.9 us
  transfers between devices with their start and end apart: 5, of which 4 were waited for; matrix products, arithmetic and copies ran while one was open for 17% of the time, Pallas kernels for 0%

commit v1 on v0

--- a/solution.py
+++ b/solution.py
@@ -1,6 +1,10 @@
+import functools
+
 import jax
 import jax.numpy as jnp
 from jax import lax
+from jax.experimental import pallas as pl
+from jax.experimental.pallas import tpu as pltpu
 from jax.sharding import PartitionSpec as P
 
 CAP = 2
@@ -19,7 +23,7 @@
     return (table, used, ranked)
 
 
-def on_device(
+def on_device_plain(
     tokens,
     value_matrix,
     adapter_down_factors,
@@ -118,6 +122,443 @@
     return (values_feature_major, tokens_grad, down_grad, up_grad)
 
 
+MESH = pl.DeviceIdType.MESH
+F32, BF16 = jnp.float32, jnp.bfloat16
+TILE = 512
+
+
+def product(a, b, left, right):
+    return lax.dot_general(a, b, (((left,), (right,)), ((), ())), preferred_element_type=F32)
+
+
+def fused_kernel(
+    groups,
+    shards,
+    table,
+    x_hbm,
+    w_hbm,
+    a_hbm,
+    b_hbm,
+    cot_hbm,
+    values_ref,
+    xgrad_hbm,
+    down_ref,
+    up_ref,
+    x,
+    weights,
+    downs,
+    ups,
+    cot,
+    back_parts,
+    low_parts,
+    back,
+    packed,
+    down_send,
+    down_got,
+    base,
+    base_send,
+    base_got,
+    up_send,
+    up_got,
+    xgrad,
+    local_sem,
+    chain_send,
+    chain_recv,
+    side_send,
+    side_recv,
+    ups_send,
+    ups_recv,
+    model_send,
+    model_recv,
+    grad_send,
+    grad_recv,
+):
+    part = lax.axis_index("parts")
+    here = lax.axis_index("grp")
+    place = lax.axis_index("fsdp")
+    rows, dcols = x.shape
+    per_owner = b_hbm.shape[0]
+    rank = b_hbm.shape[1]
+    columns = cot_hbm.shape[0]
+    blocks = rows // BLK
+    slot_rows = CAP * rank
+    group_ids = [lax.rem(here + k, groups) for k in range(groups)]
+    place_ids = [lax.rem(place + k, shards) for k in range(shards)]
+
+    own_w, own_a = w_hbm.shape[0], a_hbm.shape[0]
+    loads = [
+        pltpu.make_async_copy(b_hbm, ups.at[pl.ds(here * per_owner, per_owner)], local_sem.at[0]),
+        pltpu.make_async_copy(cot_hbm, cot.at[place], local_sem.at[1]),
+        pltpu.make_async_copy(w_hbm, weights.at[pl.ds(here * own_w, own_w)], local_sem.at[2]),
+        pltpu.make_async_copy(a_hbm, downs.at[pl.ds(here * own_a, own_a)], local_sem.at[3]),
+        pltpu.make_async_copy(x_hbm, x, local_sem.at[4]),
+    ]
+    for load in loads:
+        load.start()
+
+    barrier = pltpu.get_barrier_semaphore()
+    pl.semaphore_signal(barrier, inc=1, device_id={"parts": 1 - part}, device_id_type=MESH)
+    for other in group_ids[1:]:
+        pl.semaphore_signal(barrier, inc=1, device_id={"grp": other}, device_id_type=MESH)
+    for other in place_ids[1:]:
+        pl.semaphore_signal(barrier, inc=1, device_id={"fsdp": other}, device_id_type=MESH)
+    pl.semaphore_wait(barrier, groups + shards - 1)
+
+    stocks = ((weights, own_w), (downs, own_a))
+
+    def half(which, owner, part_of):
+        stock, own = stocks[which]
+        return stock.at[pl.ds(owner * own + part_of * (own // 2), own // 2)]
+
+    def chain(which, owner, up, step):
+        piece = half(which, owner, part)
+        return pltpu.make_async_remote_copy(
+            src_ref=piece,
+            dst_ref=piece,
+            send_sem=chain_send.at[which, up, step],
+            recv_sem=chain_recv.at[which, owner],
+            device_id={"grp": here + 1 if up else here - 1},
+            device_id_type=MESH,
+        )
+
+    def side(which, owner, part_of):
+        piece = half(which, owner, part_of)
+        return pltpu.make_async_remote_copy(
+            src_ref=piece,
+            dst_ref=piece,
+            send_sem=side_send.at[which, owner],
+            recv_sem=side_recv.at[which, owner],
+            device_id={"parts": 1 - part},
+            device_id_type=MESH,
+        )
+
+    def each_end(act):
+        @pl.when(here < groups - 1)
+        def _():
+            act(1)
+
+        @pl.when(here > 0)
+        def _():
+            act(0)
+
+    def arrived(which, step):
+        for up in (1, 0):
+            owner = here - step if up else here + step
+            valid = here >= step if up else here < groups - step
+            onward = here < groups - 1 if up else here > 0
+
+            @pl.when(valid)
+            def _():
+                chain(which, owner, up, step).wait_recv()
+
+                @pl.when(onward)
+                def _():
+                    chain(which, owner, up, step).start()
+
+                side(which, owner, part).start()
+
+    def ups_copy(k, owner):
+        piece = ups.at[pl.ds(owner * per_owner, per_owner)]
+        return pltpu.make_async_remote_copy(
+            src_ref=piece,
+            dst_ref=piece,
+            send_sem=ups_send.at[k],
+            recv_sem=ups_recv.at[owner],
+            device_id={"grp": group_ids[k]},
+            device_id_type=MESH,
+        )
+
+    def model_copy(kind, k, source, target, slot):
+        return pltpu.make_async_remote_copy(
+            src_ref=source,
+            dst_ref=target,
+            send_sem=model_send.at[kind, k],
+            recv_sem=model_recv.at[kind, slot],
+            device_id={"fsdp": place_ids[k]},
+            device_id_type=MESH,
+        )
+
+    def share(kind, buffer):
+        for k in range(1, shards):
+            model_copy(kind, k, buffer.at[place], buffer.at[place], place).start()
+
+    def shared(kind, buffer):
+        for k in range(1, shards):
+            other = place_ids[k]
+            model_copy(kind, k, buffer.at[other], buffer.at[other], other).wait_recv()
+
+    def grad_copy(kind, k, send, got, slot):
+        return pltpu.make_async_remote_copy(
+            src_ref=send.at[pl.ds(k * slot_rows, slot_rows)],
+            dst_ref=got.at[slot],
+            send_sem=grad_send.at[kind, k],
+            recv_sem=grad_recv.at[kind, slot],
+            device_id={"grp": group_ids[k]},
+            device_id_type=MESH,
+        )
+
+    loads[0].wait()
+    for k in range(1, groups):
+        ups_copy(k, here).start()
+    loads[1].wait()
+    share(0, cot)
+    for which in range(2):
+        loads[2 + which].wait()
+        each_end(lambda up: chain(which, here, up, 0).start())
+
+    adapter = [table[here * blocks + b] for b in range(blocks)]
+    position = []
+    for b in range(blocks):
+        owner = lax.div(adapter[b], per_owner)
+        before = jnp.int32(0)
+        for j in range(per_owner):
+            candidate = owner * per_owner + j
+            held = jnp.int32(0)
+            for other in range(blocks):
+                held = jnp.maximum(held, jnp.where(adapter[other] == candidate, 1, 0))
+            before = before + jnp.where(candidate < adapter[b], held, 0)
+        position.append(owner * CAP + before)
+    token_block = lax.broadcasted_iota(jnp.int32, (rank, rows), 1) // BLK
+    token_slot = jnp.zeros((rank, rows), jnp.int32)
+    for b in range(blocks):
+        token_slot = jnp.where(token_block == b, position[b], token_slot)
+
+    def pack(state):
+        for k in range(groups):
+            for c in range(CAP):
+                kept = jnp.where(token_slot == group_ids[k] * CAP + c, state, 0.0)
+                packed[pl.ds(k * slot_rows + c * rank, rank), :] = kept.astype(BF16)
+
+    for k in range(1, groups):
+        ups_copy(k, group_ids[k]).wait_recv()
+    for b in range(blocks):
+        span = pl.ds(b * BLK, BLK)
+        back_parts[place, :, span] = product(ups[adapter[b]], cot[place, :, span], 1, 0)
+    share(1, back_parts)
+    loads[4].wait()
+    shared(1, back_parts)
+    back_sum = back_parts[0]
+    for k in range(1, shards):
+        back_sum = back_sum + back_parts[k]
+    back_now = (adapter_scale * back_sum).astype(BF16)
+    back[...] = back_now
+    pack(back_now.astype(F32))
+
+    arrived(0, 1)
+
+    @pl.loop(0, dcols // TILE)
+    def _(t):
+        span = pl.ds(pl.multiple_of(t * TILE, TILE), TILE)
+        down_send[:, span] = product(packed[...], x[:, span], 1, 0).astype(BF16)
+
+    down_got[here] = down_send[:slot_rows]
+
+    def send_down():
+        for k in range(1, groups):
+            grad_copy(0, k, down_send, down_got, here).start()
+
+    arrived(1, 1)
+    send_down()
+    for step in range(2, groups):
+        arrived(0, step)
+        arrived(1, step)
+
+    def side_wait(which):
+        for k in range(1, groups):
+            side(which, group_ids[k], 1 - part).wait_recv()
+
+    side_wait(0)
+    base[...] = jnp.zeros_like(base)
+
+    @pl.loop(0, dcols // TILE)
+    def _(t):
+        span = pl.ds(pl.multiple_of(t * TILE, TILE), TILE)
+        base[...] += product(x[:, span], weights[span, :], 1, 0)
+
+    for k in range(shards):
+        base_send[k] = base[:, k * columns : (k + 1) * columns].astype(BF16)
+    for k in range(1, shards):
+        model_copy(2, k, base_send.at[place_ids[k]], base_got.at[place], place).start()
+
+    side_wait(1)
+    for b in range(blocks):
+        span = pl.ds(b * BLK, BLK)
+        low_parts[place, :, span] = product(downs[adapter[b]], x[span, :], 1, 1)
+    share(3, low_parts)
+
+    shared(0, cot)
+
+    @pl.loop(0, dcols // TILE)
+    def _(t):
+        span = pl.ds(pl.multiple_of(t * TILE, TILE), TILE)
+        whole = cot[...].reshape(shards * columns, rows)
+        from_base = product(whole, weights[span, :], 0, 1)
+        for b in range(blocks):
+            rows_b = pl.ds(b * BLK, BLK)
+            from_low = product(back[:, rows_b], downs[adapter[b], :, span], 0, 0)
+            xgrad[rows_b, span] = (from_base[b * BLK : (b + 1) * BLK] + from_low).astype(BF16)
+
+    xgrad_copy = pltpu.make_async_copy(xgrad, xgrad_hbm, local_sem.at[5])
+    xgrad_copy.start()
+
+    shared(3, low_parts)
+    low_sum = low_parts[0]
+    for k in range(1, shards):
+        low_sum = low_sum + low_parts[k]
+    low = low_sum.astype(BF16)
+    pack(low.astype(F32))
+    up_send[...] = (adapter_scale * product(packed[...], cot[place], 1, 1)).astype(BF16)
+    for k in range(1, groups):
+        grad_copy(1, k, up_send, up_got, here).start()
+    up_got[here] = up_send[:slot_rows]
+
+    for k in range(1, shards):
+        other = place_ids[k]
+        model_copy(2, k, base_send.at[other], base_got.at[other], other).wait_recv()
+    total = base[:, pl.ds(pl.multiple_of(place * columns, columns), columns)]
+    for k in range(1, shards):
+        total = total + base_got[place_ids[k]].astype(F32)
+    total = total.T
+    for b in range(blocks):
+        span = pl.ds(b * BLK, BLK)
+        added = product(ups[adapter[b]], low[:, b * BLK : (b + 1) * BLK], 0, 0)
+        values_ref[:, span] = (total[:, b * BLK : (b + 1) * BLK] + adapter_scale * added).astype(BF16)
+
+    width = groups * slot_rows
+    row = lax.broadcasted_iota(jnp.int32, (rank, width), 0)
+    lane = lax.broadcasted_iota(jnp.int32, (rank, width), 1)
+    diagonal = row == lane % rank
+    slot = lane // rank
+    chosen = []
+    befores = [jnp.int32(0)] * groups
+    for j in range(per_owner):
+        wanted = jnp.zeros((rank, width), F32)
+        for g in range(groups):
+            held = jnp.int32(0)
+            for b in range(blocks):
+                held = jnp.maximum(held, jnp.where(table[g * blocks + b] == here * per_owner + j, 1, 0))
+            at = jnp.where(held > 0, g * CAP + befores[g], -1)
+            wanted = jnp.where(slot == at, 1.0, wanted)
+            befores[g] = befores[g] + held
+        chosen.append(jnp.where(diagonal, wanted, 0.0).astype(BF16))
+    chosen = jnp.concatenate(chosen, axis=0)
+
+    for k in range(1, groups):
+        grad_copy(1, k, up_send, up_got, group_ids[k]).wait_recv()
+    got = up_got[...].reshape(width, columns)
+    up_ref[...] = product(chosen, got, 1, 0).reshape(up_ref.shape)
+    for k in range(1, groups):
+        grad_copy(0, k, down_send, down_got, group_ids[k]).wait_recv()
+    for t in range(dcols // TILE):
+        span = slice(t * TILE, (t + 1) * TILE)
+        got = down_got[:, :, span].reshape(width, TILE)
+        summed = product(chosen, got, 1, 0).astype(BF16)
+        down_ref[:, :, span] = summed.reshape(per_owner, rank, TILE)
+
+    for which in range(2):
+        each_end(lambda up: chain(which, here, up, 0).wait_send())
+        for step in range(1, groups):
+            for up in (1, 0):
+                owner = here - step if up else here + step
+                valid = here >= step if up else here < groups - step
+                onward = here < groups - 1 if up else here > 0
+
+                @pl.when(valid)
+                def _():
+                    @pl.when(onward)
+                    def _():
+                        chain(which, owner, up, step).wait_send()
+
+                    side(which, owner, part).wait_send()
+
+    for k in range(1, groups):
+        ups_copy(k, here).wait_send()
+        grad_copy(0, k, down_send, down_got, here).wait_send()
+        grad_copy(1, k, up_send, up_got, here).wait_send()
+    for k in range(1, shards):
+        for kind, buffer in ((0, cot), (1, back_parts), (3, low_parts)):
+            model_copy(kind, k, buffer.at[place], buffer.at[place], place).wait_send()
+        model_copy(2, k, base_send.at[place_ids[k]], base_got.at[place], place).wait_send()
+    xgrad_copy.wait()
+
+
+def on_device_fused(
+    tokens,
+    value_matrix,
+    adapter_down_factors,
+    adapter_up_factors,
+    block_adapter_index,
+    cotangent_feature_major,
+):
+    groups, shards = lax.axis_size("grp"), lax.axis_size("fsdp")
+    rows, dcols = tokens.shape
+    per_owner, rank, _ = adapter_down_factors.shape
+    columns = cotangent_feature_major.shape[0]
+    slot_rows = CAP * rank
+    here = pl.BlockSpec(memory_space=pltpu.VMEM)
+    away = pl.BlockSpec(memory_space=pl.ANY)
+    sems = pltpu.SemaphoreType.DMA
+    return pl.pallas_call(
+        functools.partial(fused_kernel, groups, shards),
+        out_shape=(
+            jax.ShapeDtypeStruct((columns, rows), BF16),
+            jax.ShapeDtypeStruct((rows, dcols), BF16),
+            jax.ShapeDtypeStruct((per_owner, rank, dcols), BF16),
+            jax.ShapeDtypeStruct((per_owner, rank, columns), F32),
+        ),
+        in_specs=[pl.BlockSpec(memory_space=pltpu.SMEM)] + [away] * 5,
+        out_specs=(here, away, here, here),
+        scratch_shapes=[
+            pltpu.VMEM((rows, dcols), BF16),
+            pltpu.VMEM((groups * value_matrix.shape[0], value_matrix.shape[1]), BF16),
+            pltpu.VMEM((groups * per_owner, rank, dcols), BF16),
+            pltpu.VMEM((groups * per_owner, rank, columns), BF16),
+            pltpu.VMEM((shards, columns, rows), BF16),
+            pltpu.VMEM((shards, rank, rows), F32),
+            pltpu.VMEM((shards, rank, rows), F32),
+            pltpu.VMEM((rank, rows), BF16),
+            pltpu.VMEM((groups * slot_rows, rows), BF16),
+            pltpu.VMEM((groups * slot_rows, dcols), BF16),
+            pltpu.VMEM((groups, slot_rows, dcols), BF16),
+            pltpu.VMEM((rows, shards * columns), F32),
+            pltpu.VMEM((shards, rows, columns), BF16),
+            pltpu.VMEM((shards, rows, columns), BF16),
+            pltpu.VMEM((groups * slot_rows, columns), BF16),
+            pltpu.VMEM((groups, slot_rows, columns), BF16),
+            pltpu.VMEM((rows, dcols), BF16),
+            sems((6,)),
+            sems((2, 2, groups)),
+            sems((2, groups)),
+            sems((2, groups)),
+            sems((2, groups)),
+            sems((groups,)),
+            sems((groups,)),
+            sems((4, shards)),
+            sems((4, shards)),
+            sems((2, groups)),
+            sems((2, groups)),
+        ],
+        compiler_params=pltpu.CompilerParams(
+            collective_id=0, has_side_effects=True, vmem_limit_bytes=48 * 1024 * 1024
+        ),
+    )(
+        block_adapter_index,
+        tokens,
+        value_matrix,
+        adapter_down_factors,
+        adapter_up_factors,
+        cotangent_feature_major,
+    )
+
+
+def on_device(*arrays):
+    columns, dcols = arrays[5].shape[0], arrays[0].shape[1]
+    whole_lanes = columns % 128 == 0 and dcols % TILE == 0
+    if whole_lanes and lax.axis_size("parts") == 2:
+        return on_device_fused(*arrays)
+    return on_device_plain(*arrays)
+
+
 def solution(mesh):
     return jax.shard_map(
         on_device,

time: 253 us -> 129 us (0.51)
  Pallas kernels: 0 us -> 120 us
  waiting for transfers between devices: 115 us -> 0 us
  blocking collectives: 60.4 us -> 0 us
  matrix products: 27.8 us -> 0 us
  local copies, waits for them, and re-layouts: 23.8 us -> 8.26 us
  between operations: 13.9 us -> 0.66 us
  starting transfers between devices: 8.54 us -> 0 us
  other arithmetic: 2.56 us -> 0 us
    pallas_call x0 -> x1, Pallas kernels: none -> 120 us  [on_device_fused(): pl.pallas_call(functools.partial(fused_kernel, groups, shards), out_shape...]
    all_gather x2 -> x0, waiting for transfers between devices: 68.6 us -> none  [the longest x1 65.3 us: on_device(): lax.all_gather(adapter_down_factors, 'grp', axis=0, tiled=True)]
    all_gather x2 -> x0, blocking collectives: 45 us -> none  [the longest x1 28.5 us: on_device(): lax.all_gather(cotangent_feature_major, 'fsdp', axis=0, tiled=True)]
    all_to_all x2 -> x0, waiting for transfers between devices: 35.1 us -> none  [the longest x1 35 us: on_device(): lax.all_to_all(slot_down, 'grp', split_axis=0, concat_axis=0, tiled=True)]
    dot_general x12 -> x0, matrix products: 27.8 us -> none  [the longest x1 8.9 us: on_device(): jnp.einsum('gcj,gcrd->jrd', collector, got_grad_down, precision=lax.Preci...]
    psum x1 -> x0, blocking collectives: 15.4 us -> none  [on_device(): low_rank_state = lax.psum(low_part, 'fsdp').astype(jnp.bfloat16)]
    reshape x5 -> x0, local copies, waits for them, and re-layouts: 14.2 us -> none  [the longest x2 12.6 us: on_device(): slot_down = down_slots.reshape(groups, CAP, rank_extent, dcols)]
    reduce_scatter x1 -> x0, waiting for transfers between devices: 10.2 us -> none  [on_device(): lax.psum_scatter(lax.dot_general(columns, tokens, (((0,), (1,)), ((), ())...]
  transfers between devices with their start and end apart: 5 -> 0, of which waited for: 4 -> 0; matrix products, arithmetic and copies ran while one was open for 17% -> 0% of each run, Pallas kernels for 0% -> 0%
where the time goes in v1:
time: 129 us
  Pallas kernels  120 us (93%)
  local copies, waits for them, and re-layouts  8.26 us (6%)
    pallas_call x1, Pallas kernels, on_device_fused(): pl.pallas_call(functools.partial(fused_kernel, groups, shards), out_shape...  120 us
    unnamed x14, local copies, waits for them, and re-layouts  8.26 us

profile of v1, /device:TPU:0, one launch (start us, length us, event | category | flops | bytes accessed | tf_op | source)
XLA Modules:
  0.0 128.8 jit_solution(8707519547725090704)
XLA Ops:
  0.6 0.0 copy-start
  0.6 1.2 copy-done
  1.9 0.0 copy-start.1
  1.9 1.0 copy-done.1
  2.9 0.0 copy-start.2
  2.9 0.9 copy-done.2
  3.8 0.0 copy-start.3
  3.8 0.8 copy-done.3
  4.6 0.0 copy-start.4
  4.6 0.7 copy-done.4
  5.3 119.9 %shard_map.93 = (bf16[128,512]{1,0:T(8,128)(2,1)S(1)}, bf16[512,2048]{1,0:T(8,128)(2,1)S(1)}, bf16[4,64,2048]{2,1,0:T(8,128)(2,1)S(1)}, f32[4,64,128]{2,1,0:T(8,128)S(1)}) custom-call(s32[16]{0:T(128)S(1)} %copy-done.4, bf16[512,2048]{1,0:T(8,128)(2,1)} %x_hbm.1, bf16[512,512]{1,0:T(8,128)(2,1)S(1)} %copy-done.1, bf16[4,64,2048]{2,1,0:T(8,128)(2,1)S(1)} %copy-done, ...), custom_call_target="tpu_custom_call" | custom-call | tf_op jit(solution)/shard_map/pallas_call | solution.py:501
  125.2 0.7 copy.14
  125.8 1.3 %copy.15 = bf16[512,2048]{1,0:T(8,128)(2,1)} copy(bf16[512,2048]{1,0:T(8,128)(2,1)S(1)} %get-tuple-element.9) | data formatting | bytes 4194304
  127.2 1.0 copy.16
  128.1 0.7 copy.17
Async XLA Ops:
  0.6 1.2 copy-start
  1.9 1.0 copy-start.1
  2.9 0.9 copy-start.2
  3.8 0.8 copy-start.3
  4.6 0.7 copy-start.4

commit v2 on v1

--- a/solution.py
+++ b/solution.py
@@ -204,11 +204,13 @@
         pl.semaphore_signal(barrier, inc=1, device_id={"fsdp": other}, device_id_type=MESH)
     pl.semaphore_wait(barrier, groups + shards - 1)
 
-    stocks = ((weights, own_w), (downs, own_a))
+    stocks = ((weights, own_w, 0, own_w // 2),) + tuple(
+        (downs, own_a, j, 1) for j in range(own_a // 2)
+    )
 
     def half(which, owner, part_of):
-        stock, own = stocks[which]
-        return stock.at[pl.ds(owner * own + part_of * (own // 2), own // 2)]
+        stock, own, first, count = stocks[which]
+        return stock.at[pl.ds(owner * own + part_of * (own // 2) + first, count)]
 
     def chain(which, owner, up, step):
         piece = half(which, owner, part)
@@ -302,8 +304,9 @@
         ups_copy(k, here).start()
     loads[1].wait()
     share(0, cot)
-    for which in range(2):
-        loads[2 + which].wait()
+    for which in range(len(stocks)):
+        if which < 2:
+            loads[2 + which].wait()
         each_end(lambda up: chain(which, here, up, 0).start())
 
     adapter = [table[here * blocks + b] for b in range(blocks)]
@@ -353,15 +356,22 @@
 
     down_got[here] = down_send[:slot_rows]
 
-    def send_down():
-        for k in range(1, groups):
-            grad_copy(0, k, down_send, down_got, here).start()
-
-    arrived(1, 1)
-    send_down()
+    def send_down(step):
+        @pl.when(here < groups - step)
+        def _():
+            grad_copy(0, step, down_send, down_got, here).start()
+
+        @pl.when(here >= step)
+        def _():
+            grad_copy(0, groups - step, down_send, down_got, here).start()
+
+    for which in range(1, len(stocks)):
+        arrived(which, 1)
+    send_down(1)
     for step in range(2, groups):
-        arrived(0, step)
-        arrived(1, step)
+        for which in range(len(stocks)):
+            arrived(which, step)
+        send_down(step)
 
     def side_wait(which):
         for k in range(1, groups):
@@ -380,7 +390,8 @@
     for k in range(1, shards):
         model_copy(2, k, base_send.at[place_ids[k]], base_got.at[place], place).start()
 
-    side_wait(1)
+    for which in range(1, len(stocks)):
+        side_wait(which)
     for b in range(blocks):
         span = pl.ds(b * BLK, BLK)
         low_parts[place, :, span] = product(downs[adapter[b]], x[span, :], 1, 1)
@@ -455,7 +466,7 @@
         summed = product(chosen, got, 1, 0).astype(BF16)
         down_ref[:, :, span] = summed.reshape(per_owner, rank, TILE)
 
-    for which in range(2):
+    for which in range(len(stocks)):
         each_end(lambda up: chain(which, here, up, 0).wait_send())
         for step in range(1, groups):
             for up in (1, 0):
@@ -527,10 +538,10 @@
             pltpu.VMEM((groups, slot_rows, columns), BF16),
             pltpu.VMEM((rows, dcols), BF16),
             sems((6,)),
-            sems((2, 2, groups)),
-            sems((2, groups)),
-            sems((2, groups)),
-            sems((2, groups)),
+            sems((1 + per_owner // 2, 2, groups)),
+            sems((1 + per_owner // 2, groups)),
+            sems((1 + per_owner // 2, groups)),
+            sems((1 + per_owner // 2, groups)),
             sems((groups,)),
             sems((groups,)),
             sems((4, shards)),
@@ -539,7 +550,7 @@
             sems((2, groups)),
         ],
         compiler_params=pltpu.CompilerParams(
-            collective_id=0, has_side_effects=True, vmem_limit_bytes=48 * 1024 * 1024
+            collective_id=0, has_side_effects=True, vmem_limit_bytes=63 * 1024 * 1024
         ),
     )(
         block_adapter_index,

time: 129 us -> 113 us (0.88)
  Pallas kernels: 120 us -> 105 us
  local copies, waits for them, and re-layouts: 8.26 us -> 6.45 us
    pallas_call x1, Pallas kernels: 120 us -> 105 us  [on_device_fused(): pl.pallas_call(functools.partial(fused_kernel, groups, shards), out_shape...]
    unnamed x14 -> x8, local copies, waits for them, and re-layouts: 8.26 us -> 6.45 us
where the time goes in v2:
time: 113 us; the launch traced here: 112 us
  Pallas kernels  105 us (93%)
  local copies, waits for them, and re-layouts  6.45 us (6%)
    pallas_call x1, Pallas kernels, on_device_fused(): pl.pallas_call(functools.partial(fused_kernel, groups, shards), out_shape...  105 us
    unnamed x8, local copies, waits for them, and re-layouts  6.45 us

profile of v2, /device:TPU:0, one launch (start us, length us, event | category | flops | bytes accessed | tf_op | source)
XLA Modules:
  0.0 111.9 jit_solution(17635579849039772592)
XLA Ops:
  0.6 104.8 %shard_map.93 = (bf16[128,512]{1,0:T(8,128)(2,1)}, bf16[512,2048]{1,0:T(8,128)(2,1)}, bf16[4,64,2048]{2,1,0:T(8,128)(2,1)}, f32[4,64,128]{2,1,0:T(8,128)}) custom-call(s32[16]{0:T(128)} %table.1, bf16[512,2048]{1,0:T(8,128)(2,1)} %x_hbm.1, bf16[512,512]{1,0:T(8,128)(2,1)} %w_hbm.1, bf16[4,64,2048]{2,1,0:T(8,128)(2,1)} %a_hbm.1, bf16[4,64,128]{2,1,0:T(8,128)(2,1)} %b_hbm.1, ...), custom_call_target="tpu_custom_call" | custom-call | tf_op jit(solution)/shard_map/pallas_call | solution.py:512
  105.4 1.6 %copy.14 = bf16[128,512]{1,0:T(8,128)(2,1)} copy(bf16[128,512]{1,0:T(8,128)(2,1)} %get-tuple-element.8) | data formatting | bytes 262144
  107.0 0.0 copy-start
  107.0 0.0 copy-start.1
  107.0 3.3 %copy.15 = bf16[512,2048]{1,0:T(8,128)(2,1)} copy(bf16[512,2048]{1,0:T(8,128)(2,1)} %get-tuple-element.9) | data formatting | bytes 4194304
  110.3 0.0 copy-done
  110.3 1.0 copy.16
  111.2 0.0 copy-done.1
  111.2 0.7 copy.17
Async XLA Ops:
  107.0 3.3 %copy-start = (bf16[4,64,2048]{2,1,0:T(8,128)(2,1)S(1)}, bf16[4,64,2048]{2,1,0:T(8,128)(2,1)}, u32[]{:S(2)}) copy-start(bf16[4,64,2048]{2,1,0:T(8,128)(2,1)} %get-tuple-element.10) | copy-start | bytes 3145732
  107.0 4.2 %copy-start.1 = (f32[4,64,128]{2,1,0:T(8,128)S(1)}, f32[4,64,128]{2,1,0:T(8,128)}, u32[]{:S(2)}) copy-start(f32[4,64,128]{2,1,0:T(8,128)} %get-tuple-element.11) | copy-start | bytes 393220

commit v3 on v2

--- a/solution.py
+++ b/solution.py
@@ -302,12 +302,13 @@
     loads[0].wait()
     for k in range(1, groups):
         ups_copy(k, here).start()
+    def begin(which):
+        each_end(lambda up: chain(which, here, up, 0).start())
+
+    loads[2].wait()
+    begin(0)
     loads[1].wait()
-    share(0, cot)
-    for which in range(len(stocks)):
-        if which < 2:
-            loads[2 + which].wait()
-        each_end(lambda up: chain(which, here, up, 0).start())
+    loads[3].wait()
 
     adapter = [table[here * blocks + b] for b in range(blocks)]
     position = []
@@ -338,6 +339,9 @@
         span = pl.ds(b * BLK, BLK)
         back_parts[place, :, span] = product(ups[adapter[b]], cot[place, :, span], 1, 0)
     share(1, back_parts)
+    begin(1)
+    arrived(0, 1)
+    share(0, cot)
     loads[4].wait()
     shared(1, back_parts)
     back_sum = back_parts[0]
@@ -347,7 +351,10 @@
     back[...] = back_now
     pack(back_now.astype(F32))
 
-    arrived(0, 1)
+    for which in range(2, len(stocks)):
+        begin(which)
+    if groups > 2:
+        arrived(0, 2)
 
     @pl.loop(0, dcols // TILE)
     def _(t):
@@ -365,13 +372,11 @@
         def _():
             grad_copy(0, groups - step, down_send, down_got, here).start()
 
-    for which in range(1, len(stocks)):
+    arrived(1, 1)
+    for step in range(3, groups):
+        arrived(0, step)
+    for which in range(2, len(stocks)):
         arrived(which, 1)
-    send_down(1)
-    for step in range(2, groups):
-        for which in range(len(stocks)):
-            arrived(which, step)
-        send_down(step)
 
     def side_wait(which):
         for k in range(1, groups):
@@ -389,6 +394,12 @@
         base_send[k] = base[:, k * columns : (k + 1) * columns].astype(BF16)
     for k in range(1, shards):
         model_copy(2, k, base_send.at[place_ids[k]], base_got.at[place], place).start()
+
+    for step in range(2, groups):
+        for which in range(1, len(stocks)):
+            arrived(which, step)
+        send_down(step - 1)
+    send_down(groups - 1)
 
     for which in range(1, len(stocks)):
         side_wait(which)

time: 113 us -> 110 us (0.973)
  Pallas kernels: 105 us -> 103 us
    pallas_call x1, Pallas kernels: 105 us -> 103 us  [on_device_fused(): pl.pallas_call(functools.partial(fused_kernel, groups, shards), out_shape...]
where the time goes in v3:
time: 110 us
  Pallas kernels  103 us (94%)
  local copies, waits for them, and re-layouts  6.45 us (6%)
    pallas_call x1, Pallas kernels, on_device_fused(): pl.pallas_call(functools.partial(fused_kernel, groups, shards), out_shape...  103 us
    unnamed x8, local copies, waits for them, and re-layouts  6.45 us

profile of v3, /device:TPU:0, one launch (start us, length us, event | category | flops | bytes accessed | tf_op | source)
XLA Modules:
  0.0 110.0 jit_solution(17000329752793335677)
XLA Ops:
  0.6 102.9 %shard_map.93 = (bf16[128,512]{1,0:T(8,128)(2,1)}, bf16[512,2048]{1,0:T(8,128)(2,1)}, bf16[4,64,2048]{2,1,0:T(8,128)(2,1)}, f32[4,64,128]{2,1,0:T(8,128)}) custom-call(s32[16]{0:T(128)} %table.1, bf16[512,2048]{1,0:T(8,128)(2,1)} %x_hbm.1, bf16[512,512]{1,0:T(8,128)(2,1)} %w_hbm.1, bf16[4,64,2048]{2,1,0:T(8,128)(2,1)} %a_hbm.1, bf16[4,64,128]{2,1,0:T(8,128)(2,1)} %b_hbm.1, ...), custom_call_target="tpu_custom_call" | custom-call | tf_op jit(solution)/shard_map/pallas_call | solution.py:523
  103.6 1.6 %copy.14 = bf16[128,512]{1,0:T(8,128)(2,1)} copy(bf16[128,512]{1,0:T(8,128)(2,1)} %get-tuple-element.8) | data formatting | bytes 262144
  105.1 0.0 copy-start
  105.1 0.0 copy-start.1
  105.1 3.3 %copy.15 = bf16[512,2048]{1,0:T(8,128)(2,1)} copy(bf16[512,2048]{1,0:T(8,128)(2,1)} %get-tuple-element.9) | data formatting | bytes 4194304
  108.4 0.0 copy-done
  108.4 1.0 copy.16
  109.4 0.0 copy-done.1
  109.4 0.7 copy.17
Async XLA Ops:
  105.1 3.3 %copy-start = (bf16[4,64,2048]{2,1,0:T(8,128)(2,1)S(1)}, bf16[4,64,2048]{2,1,0:T(8,128)(2,1)}, u32[]{:S(2)}) copy-start(bf16[4,64,2048]{2,1,0:T(8,128)(2,1)} %get-tuple-element.10) | copy-start | bytes 3145732
  105.1 4.2 %copy-start.1 = (f32[4,64,128]{2,1,0:T(8,128)S(1)}, f32[4,64,128]{2,1,0:T(8,128)}, u32[]{:S(2)}) copy-start(f32[4,64,128]{2,1,0:T(8,128)} %get-tuple-element.11) | copy-start | bytes 393220

commit v4 on v3

--- a/solution.py
+++ b/solution.py
@@ -168,6 +168,8 @@
     side_recv,
     ups_send,
     ups_recv,
+    ups_side_send,
+    ups_side_recv,
     model_send,
     model_recv,
     grad_send,
@@ -259,8 +261,22 @@
 
                 side(which, owner, part).start()
 
+    def ups_half(owner, part_of):
+        return ups.at[pl.ds(owner * per_owner + part_of * (per_owner // 2), per_owner // 2)]
+
+    def ups_side(owner, part_of):
+        piece = ups_half(owner, part_of)
+        return pltpu.make_async_remote_copy(
+            src_ref=piece,
+            dst_ref=piece,
+            send_sem=ups_side_send.at[owner],
+            recv_sem=ups_side_recv.at[owner],
+            device_id={"parts": 1 - part},
+            device_id_type=MESH,
+        )
+
     def ups_copy(k, owner):
-        piece = ups.at[pl.ds(owner * per_owner, per_owner)]
+        piece = ups_half(owner, part)
         return pltpu.make_async_remote_copy(
             src_ref=piece,
             dst_ref=piece,
@@ -335,6 +351,9 @@
 
     for k in range(1, groups):
         ups_copy(k, group_ids[k]).wait_recv()
+        ups_side(group_ids[k], part).start()
+    for k in range(1, groups):
+        ups_side(group_ids[k], 1 - part).wait_recv()
     for b in range(blocks):
         span = pl.ds(b * BLK, BLK)
         back_parts[place, :, span] = product(ups[adapter[b]], cot[place, :, span], 1, 0)
@@ -495,6 +514,7 @@
 
     for k in range(1, groups):
         ups_copy(k, here).wait_send()
+        ups_side(group_ids[k], part).wait_send()
         grad_copy(0, k, down_send, down_got, here).wait_send()
         grad_copy(1, k, up_send, up_got, here).wait_send()
     for k in range(1, shards):
@@ -555,6 +575,8 @@
             sems((1 + per_owner // 2, groups)),
             sems((groups,)),
             sems((groups,)),
+            sems((groups,)),
+            sems((groups,)),
             sems((4, shards)),
             sems((4, shards)),
             sems((2, groups)),

time: 110 us -> 107 us (0.973)
  Pallas kernels: 103 us -> 100 us
    pallas_call x1, Pallas kernels: 103 us -> 100 us  [on_device_fused(): pl.pallas_call(functools.partial(fused_kernel, groups, shards), out_shape...]
where the time goes in v4:
time: 107 us
  Pallas kernels  100 us (93%)
  local copies, waits for them, and re-layouts  6.45 us (6%)
    pallas_call x1, Pallas kernels, on_device_fused(): pl.pallas_call(functools.partial(fused_kernel, groups, shards), out_shape...  100 us
    unnamed x8, local copies, waits for them, and re-layouts  6.45 us

profile of v4, /device:TPU:0, one launch (start us, length us, event | category | flops | bytes accessed | tf_op | source)
XLA Modules:
  0.0 107.3 jit_solution(15654101540260554918)
XLA Ops:
  0.6 100.2 %shard_map.93 = (bf16[128,512]{1,0:T(8,128)(2,1)}, bf16[512,2048]{1,0:T(8,128)(2,1)}, bf16[4,64,2048]{2,1,0:T(8,128)(2,1)}, f32[4,64,128]{2,1,0:T(8,128)}) custom-call(s32[16]{0:T(128)} %table.1, bf16[512,2048]{1,0:T(8,128)(2,1)} %x_hbm.1, bf16[512,512]{1,0:T(8,128)(2,1)} %w_hbm.1, bf16[4,64,2048]{2,1,0:T(8,128)(2,1)} %a_hbm.1, bf16[4,64,128]{2,1,0:T(8,128)(2,1)} %b_hbm.1, ...), custom_call_target="tpu_custom_call" | custom-call | tf_op jit(solution)/shard_map/pallas_call | solution.py:543
  100.9 1.6 %copy.14 = bf16[128,512]{1,0:T(8,128)(2,1)} copy(bf16[128,512]{1,0:T(8,128)(2,1)} %get-tuple-element.8) | data formatting | bytes 262144
  102.4 0.0 copy-start
  102.4 0.0 copy-start.1
  102.4 3.3 %copy.15 = bf16[512,2048]{1,0:T(8,128)(2,1)} copy(bf16[512,2048]{1,0:T(8,128)(2,1)} %get-tuple-element.9) | data formatting | bytes 4194304
  105.7 0.0 copy-done
  105.7 1.0 copy.16
  106.7 0.0 copy-done.1
  106.7 0.7 copy.17
Async XLA Ops:
  102.4 3.3 %copy-start = (bf16[4,64,2048]{2,1,0:T(8,128)(2,1)S(1)}, bf16[4,64,2048]{2,1,0:T(8,128)(2,1)}, u32[]{:S(2)}) copy-start(bf16[4,64,2048]{2,1,0:T(8,128)(2,1)} %get-tuple-element.10) | copy-start | bytes 3145732
  102.4 4.2 %copy-start.1 = (f32[4,64,128]{2,1,0:T(8,128)S(1)}, f32[4,64,128]{2,1,0:T(8,128)}, u32[]{:S(2)}) copy-start(f32[4,64,128]{2,1,0:T(8,128)} %get-tuple-element.11) | copy-start | bytes 393220
